TPU v7x, 1024 devices: a whole 8x8x8 slice. The times are simulated.
1024 devices in a mesh: pipe: 8 (over x), expert: 64 (over z, y), tensor: 2 (over core).
Axes of the slice: x: 8, y: 8, z: 8, core: 2. Of those that a mesh axis runs over, the one named last changes fastest.
Arguments:
- in_flight: bfloat16 [8, 4096, 2048], P('pipe', 'expert', 'tensor'), may hold values from -6 to 6
- fresh_batch: bfloat16 [1, 4096, 2048], P(None, 'expert', 'tensor'), may hold values from -6 to 6
- norm_gain: float32 [8, 2048], P('pipe', 'tensor'), may hold values from 0.25 to 1.75
- up_weight: bfloat16 [8, 64, 2048, 768], P('pipe', 'expert', 'tensor'), may hold values from -0.125 to 0.125
- down_weight: bfloat16 [8, 64, 768, 2048], P('pipe', 'expert', None, 'tensor'), may hold values from -0.21875 to 0.21875
- expert_ids: int32 [2, 8, 4096, 8], P(None, 'pipe', 'expert'), may hold values from 0 to 63, all different within a row; in each aligned block of 64 rows (0 to 63, 64 to 127, ..., all dimensions but the last counted through in order) at most 9 rows name the same one
- route_prob: float32 [2, 8, 4096, 8], P(None, 'pipe', 'expert'), may hold values from 0.05 to 1
Outputs:
- section_out: bfloat16 [8, 4096, 2048], P('pipe', 'expert', 'tensor')
Inputs may be any that keep to these rules, and one draw needn't show every extreme that they name: `expert_ids`: in each aligned block of 64 tokens (the tokens of one expert index in one tick and section) no expert is named by more than 9 tokens, and some blocks reach it.
All inputs are finite; a program needn't handle non-finite values.
Results may differ from a plain program's by a relative error of at most 0.023.
Values may be sent and summed in bfloat16 or wider, within the bound.
A program may use at most 32 MiB of HBM per device.

v0:
```python
import jax
import jax.numpy as jnp
from jax import lax
from jax.sharding import PartitionSpec as P

epsilon = 1e-06


def passed_along(shard, axis, by):
    peers = lax.axis_size(axis)
    pairs = [(i, i + by) for i in range(peers) if 0 <= i + by < peers]
    return lax.ppermute(shard, axis, pairs)


def slot_table(block_ids, experts_all, capacity):
    one_hot = (
        block_ids[:, :, None] == jnp.arange(experts_all, dtype=jnp.int32)[None, None, :]
    ).astype(jnp.int32)
    per_token = jnp.sum(one_hot, axis=1)
    earlier = jnp.cumsum(per_token, axis=0) - per_token
    position = jnp.take_along_axis(earlier, block_ids, axis=1)
    return block_ids * capacity + position


def run_section(current, gain_row, up_local, down_local, ids_now, prob_now):
    half_width = current.shape[1]
    full_width = half_width * lax.axis_size("tensor")
    as_float = current.astype(jnp.float32)
    squares = lax.psum(jnp.sum(as_float * as_float, axis=1), "tensor")
    scaled = (
        as_float * lax.rsqrt(squares / full_width + epsilon)[:, None] * gain_row[None, :]
    ).astype(jnp.bfloat16)
    local_count = up_local.shape[0]
    sources = lax.axis_size("expert")
    experts_all = local_count * sources
    token_count = ids_now.shape[0]
    picks = ids_now.shape[1]
    capacity = token_count * picks // experts_all + 1
    slot_index = slot_table(ids_now, experts_all, capacity)
    flat_slots = jnp.zeros((experts_all * capacity, half_width), jnp.bfloat16)
    flat_slots = flat_slots.at[slot_index.reshape(-1)].set(jnp.repeat(scaled, picks, axis=0))
    outgoing = flat_slots.reshape(experts_all, capacity, half_width)
    received = lax.all_to_all(outgoing, "expert", split_axis=0, concat_axis=0, tiled=True)
    expert_rows = received.reshape(sources, local_count, capacity, half_width)
    expert_rows = jnp.transpose(expert_rows, (1, 0, 2, 3)).reshape(
        local_count, sources * capacity, half_width
    )
    partial_up = jnp.einsum(
        "erd,edh->erh", expert_rows, up_local, preferred_element_type=jnp.float32
    )
    summed = lax.psum(partial_up.astype(jnp.bfloat16), "tensor").astype(jnp.float32)
    hidden = jax.nn.silu(summed).astype(jnp.bfloat16)
    produced = jnp.einsum(
        "erh,ehd->erd", hidden, down_local, preferred_element_type=jnp.float32
    ).astype(jnp.bfloat16)
    produced = produced.reshape(local_count, sources, capacity, half_width)
    produced = jnp.transpose(produced, (1, 0, 2, 3)).reshape(
        sources * local_count, capacity, half_width
    )
    returned = lax.all_to_all(produced, "expert", split_axis=0, concat_axis=0, tiled=True)
    picked = returned.reshape(experts_all * capacity, half_width)[slot_index]
    weights = prob_now / jnp.sum(prob_now, axis=1, keepdims=True)
    mixture = jnp.sum(weights[:, :, None] * picked.astype(jnp.float32), axis=1)
    return (as_float + mixture).astype(jnp.bfloat16)


def on_device(in_flight, fresh_batch, norm_gain, up_weight, down_weight, expert_ids, route_prob):
    leading = lax.axis_index("pipe") == 0
    current = in_flight[0]
    for tick_index in range(expert_ids.shape[0]):
        if tick_index > 0:
            arrived = passed_along(current, "pipe", 1)
            current = jnp.where(leading, fresh_batch[tick_index - 1], arrived)
        current = run_section(
            current,
            norm_gain[0],
            up_weight[0],
            down_weight[0],
            expert_ids[tick_index, 0],
            route_prob[tick_index, 0],
        )
    return current[None]


def solution(mesh):
    placed = (
        P("pipe", "expert", "tensor"),
        P(None, "expert", "tensor"),
        P("pipe", "tensor"),
        P("pipe", "expert", "tensor", None),
        P("pipe", "expert", None, "tensor"),
        P(None, "pipe", "expert", None),
        P(None, "pipe", "expert", None),
    )
    return jax.shard_map(
        on_device,
        mesh=mesh,
        in_specs=placed,
        out_specs=P("pipe", "expert", "tensor"),
        check_vma=False,
    )
```

profile of v0, /device:TPU:14, one launch (start us, length us, event | category | flops | bytes accessed | tf_op | source)
XLA Modules:
  0.0 425.9 jit_solution(9470298287578558516)
XLA Ops:
  6.5 0.0 copy-start
  6.5 0.0 all-reduce.3.cloned.1.call-start
  6.5 1.1 fusion.54
  7.7 2.5 psum.28
  10.2 0.7 fusion.61
  10.9 0.1 copy.20
  11.0 0.2 convert_reduce_fusion.1
  11.2 0.1 reduce_window_sum.17
  11.3 0.1 reshape.247
  11.3 0.0 copy-start.1
  11.4 0.0 copy-start.4
  11.4 3.8 gather_fusion.2
  15.1 0.1 reshape.250
  15.3 0.1 reshape.170
  15.4 0.0 copy-done.1
  15.4 0.0 copy-done.4
  15.4 0.1 fusion.56
  15.5 2.9 scatter_custom_fusion
  18.3 1.6 reshape.172
  20.0 76.6 %all_to_all.20 = bf16[64,9,1024]{2,1,0:T(8,128)(2,1)} all-to-all(bf16[64,9,1024]{2,1,0:T(8,128)(2,1)} %reshape.172), channel_id=1, replica_groups=mesh['pipe'=8,'expert'=64,'tensor'=2] {'expert'}, dimensions={0} | all-to-all | bytes 2359296 | tf_op jit(solution)/shard_map/all_to_all | solution.py:43
  96.5 2.5 reshape.173
  99.1 3.4 fusion.33
  102.5 0.0 all-reduce.3.cloned.1.call-update
  102.5 37.4 %all-reduce.3.cloned.1.call-done = bf16[1,576,768]{2,1,0:T(8,128)(2,1)} async-done(((bf16[1,576,768]{2,1,0:T(8,128)(2,1)}), bf16[1,576,768]{2,1,0:T(8,128)(2,1)}) %all-reduce.3.cloned.1.call-update) | async-done | bytes 884752 | tf_op jit(solution)/shard_map/psum | solution.py:51
  140.0 2.3 fusion.18
  142.2 1.5 reshape_transpose_reshape.8
  143.8 14.4 %all-to-all-start.1 = ((bf16[64,9,1024]{2,1,0:T(8,128)(2,1)}), bf16[64,9,1024]{2,1,0:T(8,128)(2,1)}, u32[]{:S(2)}, u32[]{:S(2)}) async-start(bf16[64,9,1024]{2,1,0:T(8,128)(2,1)} %reshape_transpose_reshape.8), calls=%async_computation.1 | async-start | bytes 4194304 | tf_op jit(solution)/shard_map/all_to_all | solution.py:60
  158.2 0.0 all-reduce.5.cloned.1.call-start
  158.2 0.1 copy.21
  158.3 0.2 convert_reduce_fusion
  158.5 0.1 reduce_window_sum.18
  158.6 0.1 reshape.252
  158.7 0.0 copy-start.3
  158.7 3.8 gather_fusion.3
  162.5 0.1 reshape.255
  162.6 0.1 reshape.178
  162.7 0.1 reshape.200
  162.8 0.1 copy.16
  162.9 48.2 %all-to-all-done.1 = bf16[64,9,1024]{2,1,0:T(8,128)(2,1)} async-done(((bf16[64,9,1024]{2,1,0:T(8,128)(2,1)}), bf16[64,9,1024]{2,1,0:T(8,128)(2,1)}, u32[]{:S(2)}, u32[]{:S(2)}) %all-to-all-start.1) | async-done | bytes 1179680 | tf_op jit(solution)/shard_map/all_to_all | solution.py:60
  211.1 2.5 reshape.177
  213.7 2.8 gather_fusion
  216.5 2.0 fusion.1
  218.5 1.3 collective-permute-start
  219.8 5.5 %collective-permute-done = bf16[64,1024]{1,0:T(8,128)(2,1)S(1)} collective-permute-done((bf16[64,1024]{1,0:T(8,128)(2,1)S(1)}, bf16[64,1024]{1,0:T(8,128)(2,1)S(1)}, u32[]{:S(2)}, u32[]{:S(2)}) %collective-permute-start) | collective-permute-done | bytes 131104 | tf_op jit(solution)/shard_map/ppermute | solution.py:12
  225.3 0.1 fusion.50
  225.5 2.6 psum.30
  228.1 0.1 fusion.52
  228.2 2.9 scatter_custom_fusion.1
  231.1 1.6 reshape.180
  232.7 62.5 %all_to_all.21 = bf16[64,9,1024]{2,1,0:T(8,128)(2,1)} all-to-all(bf16[64,9,1024]{2,1,0:T(8,128)(2,1)} %reshape.180), channel_id=1, replica_groups=mesh['pipe'=8,'expert'=64,'tensor'=2] {'expert'}, dimensions={0} | all-to-all | bytes 2359296 | tf_op jit(solution)/shard_map/all_to_all | solution.py:43
  295.2 2.5 reshape.181
  297.8 3.4 fusion.30
  301.2 0.0 all-reduce.5.cloned.1.call-update
  301.2 38.7 %all-reduce.5.cloned.1.call-done = bf16[1,576,768]{2,1,0:T(8,128)(2,1)} async-done(((bf16[1,576,768]{2,1,0:T(8,128)(2,1)}), bf16[1,576,768]{2,1,0:T(8,128)(2,1)}) %all-reduce.5.cloned.1.call-update) | async-done | bytes 884752 | tf_op jit(solution)/shard_map/psum | solution.py:51
  339.9 2.3 fusion.21
  342.2 1.5 reshape_transpose_reshape.9
  343.8 14.4 %all-to-all-start.3 = ((bf16[64,9,1024]{2,1,0:T(8,128)(2,1)}), bf16[64,9,1024]{2,1,0:T(8,128)(2,1)}, u32[]{:S(2)}, u32[]{:S(2)}) async-start(bf16[64,9,1024]{2,1,0:T(8,128)(2,1)} %reshape_transpose_reshape.9), calls=%async_computation.3 | async-start | bytes 4194304 | tf_op jit(solution)/shard_map/all_to_all | solution.py:60
  358.1 0.1 copy.18
  358.2 0.1 reshape.208
  358.3 52.7 %all-to-all-done.3 = bf16[64,9,1024]{2,1,0:T(8,128)(2,1)} async-done(((bf16[64,9,1024]{2,1,0:T(8,128)(2,1)}), bf16[64,9,1024]{2,1,0:T(8,128)(2,1)}, u32[]{:S(2)}, u32[]{:S(2)}) %all-to-all-start.3) | async-done | bytes 1179680 | tf_op jit(solution)/shard_map/all_to_all | solution.py:60
  411.1 2.5 reshape.183
  413.6 2.8 gather_fusion.1
  416.4 1.9 fusion
  418.4 0.7 fusion.58
  (19 shorter events, 0.2 us)
Async XLA Ops:
  6.5 133.4 %copy-start = (bf16[1,1,768,1024]{3,2,1,0:T(8,128)(2,1)S(1)}, bf16[1,1,768,1024]{3,2,1,0:T(8,128)(2,1)}, u32[]{:S(2)}) copy-start(bf16[1,1,768,1024]{3,2,1,0:T(8,128)(2,1)} %param.13) | copy-start | bytes 4718596
  6.5 133.4 %all-reduce.3.cloned.1.call-start = ((), (), s32[]{:S(2)}) async-start(), calls=%async_computation.4 | async-start | bytes 1769472 | tf_op jit(solution)/shard_map/psum | solution.py:51
  11.3 4.0 copy-start.1
  11.4 4.0 copy-start.4
  143.8 67.3 %all-to-all-start.1 = ((bf16[64,9,1024]{2,1,0:T(8,128)(2,1)}), bf16[64,9,1024]{2,1,0:T(8,128)(2,1)}, u32[]{:S(2)}, u32[]{:S(2)}) async-start(bf16[64,9,1024]{2,1,0:T(8,128)(2,1)} %reshape_transpose_reshape.8), calls=%async_computation.1 | async-start | bytes 4194304 | tf_op jit(solution)/shard_map/all_to_all | solution.py:60
  158.2 181.8 %all-reduce.5.cloned.1.call-start = ((), (), s32[]{:S(2)}) async-start(), calls=%async_computation.5 | async-start | bytes 1769472 | tf_op jit(solution)/shard_map/psum | solution.py:51
  158.7 4.1 copy-start.3
  216.5 8.9 %copy-start.2 = (bf16[1,64,1024]{2,1,0:T(8,128)(2,1)S(1)}, bf16[1,64,1024]{2,1,0:T(8,128)(2,1)}, u32[]{:S(2)}) copy-start(bf16[1,64,1024]{2,1,0:T(8,128)(2,1)} %param.10) | copy-start | bytes 393220
  218.5 6.9 %collective-permute-start = (bf16[64,1024]{1,0:T(8,128)(2,1)S(1)}, bf16[64,1024]{1,0:T(8,128)(2,1)S(1)}, u32[]{:S(2)}, u32[]{:S(2)}) collective-permute-start(bf16[64,1024]{1,0:T(8,128)(2,1)S(1)} %fusion.57), channel_id=1, source_target_pairs={{0,128},{128,256},{256,384},{384,512},{512,640},{640,768},{768,896... | collective-permute-start | bytes 393224 | tf_op jit(solution)/shard_map/ppermute | solution.py:12
  343.8 67.3 %all-to-all-start.3 = ((bf16[64,9,1024]{2,1,0:T(8,128)(2,1)}), bf16[64,9,1024]{2,1,0:T(8,128)(2,1)}, u32[]{:S(2)}, u32[]{:S(2)}) async-start(bf16[64,9,1024]{2,1,0:T(8,128)(2,1)} %reshape_transpose_reshape.9), calls=%async_computation.3 | async-start | bytes 4194304 | tf_op jit(solution)/shard_map/all_to_all | solution.py:60
Sparse Core Ops, SparseCore 0:
  102.7 37.2 all-reduce.2
  301.4 38.5 all-reduce.4
where the time goes:
time: 427 us; the launch traced here: 426 us
  waiting for transfers between devices  183 us (43%)
  blocking collectives  144 us (34%)
  local copies, waits for them, and re-layouts  37.1 us (9%)
  starting transfers between devices  30.1 us (7%)
  between operations  13.7 us (3%)
  matrix products  11.4 us (3%)
  other arithmetic  6.76 us (2%)
    all_to_all x2, blocking collectives, run_section(): lax.all_to_all(outgoing, 'expert', split_axis=0, concat_axis=0, tiled=True)  139 us
    all_to_all x2, waiting for transfers between devices, run_section(): lax.all_to_all(produced, 'expert', split_axis=0, concat_axis=0, tiled=True)  101 us
    psum x2, waiting for transfers between devices, run_section(): lax.psum(partial_up.astype(jnp.bfloat16), 'tensor').astype(jnp.float32)  76.1 us
    all_to_all x2, starting transfers between devices, run_section(): lax.all_to_all(produced, 'expert', split_axis=0, concat_axis=0, tiled=True)  28.8 us
  transfers between devices with their start and end apart: 5, of which 5 were waited for; matrix products, arithmetic and copies ran while one was open for 1% of the time, Pallas kernels for 0%

commit v1 on v0

v1 whole, which is shorter than its diff:
```python
import functools
import jax
import jax.numpy as jnp
from jax import lax
import jax.experimental.pallas as pl
import jax.experimental.pallas.tpu as pltpu
from jax.sharding import PartitionSpec as P

EPS = 1e-06
MESH = pl.DeviceIdType.MESH
F32 = jnp.float32
BF16 = jnp.bfloat16

SIDE = 8
TOK = 64
TOPK = 8
D = 1024
HID = 768
HC = 3
HW = HID // HC
NC = 2
C = D // NC
C2 = C // 2
TICKS = 2

OFFSETS = (0, 1, 7, 2, 6, 3, 5, 4)
POS = {j: p for p, j in enumerate(OFFSETS)}
PARENT = {1: 0, 2: 1, 3: 2, 4: 3, 7: 0, 6: 7, 5: 6}
CHILDREN = {j: tuple(c for c in PARENT if PARENT[c] == j) for j in range(SIDE)}
ARRIVALS = ((1, 7), (2, 6), (3, 5), (4,))


def offset_of(position):
    odd = lax.rem(position, 2) == 1
    return jnp.where(odd, (position + 1) // 2, lax.rem(SIDE - position // 2, SIDE))


def dot(a, b):
    return jnp.dot(a, b, preferred_element_type=F32)


def kernel(
    x_ref, fresh_ref, gain_ref, up_hbm, down_hbm, ids_ref, prob_ref, out_ref,
    wup, wdn, gb, mb, xb, rb, rxb, pacc, ps, pr, hid, ob, oxb, tb, txb, sb, rr,
    sqs, sqr, shs, shr, xn, ms, mr, omat, o8, got, g8t,
    wsem, meta_sem, sq_sem, sh_send, sh_recv, ring_send, ring_recv, main_sem, ext_sem,
    p_sem, rmain_sem, rext_sem, back_send, back_recv,
):
    core = lax.axis_index("tensor")
    expert = lax.axis_index("expert")
    pipe = lax.axis_index("pipe")
    ez, ey = expert // SIDE, lax.rem(expert, SIDE)
    a = (1 - core) * ez + core * ey
    b = (1 - core) * ey + core * ez

    def device_at(da, db):
        ta, tb_ = lax.rem(a + da + SIDE, SIDE), lax.rem(b + db + SIDE, SIDE)
        return {"expert": (1 - core) * (ta * SIDE + tb_) + core * (tb_ * SIDE + ta)}

    def first(da):
        return device_at(da, 0)

    def second(db):
        return device_at(0, db)

    def remote(src, dst, send, recv, device):
        return pltpu.make_async_remote_copy(
            src_ref=src, dst_ref=dst, send_sem=send, recv_sem=recv,
            device_id=device, device_id_type=MESH,
        )

    up_copy = pltpu.make_async_copy(up_hbm, wup, wsem.at[0])
    down_copy = pltpu.make_async_copy(down_hbm, wdn, wsem.at[1])
    up_copy.start()
    down_copy.start()

    barrier = pltpu.get_barrier_semaphore()
    other_core = {"tensor": 1 - core}

    def greet(device):
        pl.semaphore_signal(barrier, inc=1, device_id=device, device_id_type=MESH)

    for d in range(1, SIDE):
        greet(first(d))
        greet(second(d))
    greet(other_core)

    @pl.when(pipe > 0)
    def _():
        greet({"pipe": pipe - 1})

    @pl.when(pipe < lax.axis_size("pipe") - 1)
    def _():
        greet({"pipe": pipe + 1})

    def put_squares(t, x):
        sums = jnp.sum(x * x, axis=1, keepdims=True)
        sqs[t] = jnp.broadcast_to(sums, (TOK, 128))

    def squares_copy(t):
        return remote(sqs.at[t], sqr.at[t], sq_sem.at[t, 0], sq_sem.at[t, 1], other_core)

    def make_meta():
        row = lax.broadcasted_iota(jnp.int32, (SIDE * SIDE, 128), 0)
        ta = lax.rem(a + row // SIDE, SIDE)
        tb_ = lax.rem(b + offset_of(lax.rem(row, SIDE)), SIDE)
        named = (1 - core) * (ta * SIDE + tb_) + core * (tb_ * SIDE + ta)
        r128 = lax.broadcasted_iota(jnp.int32, (128, 128), 0)
        l128 = lax.broadcasted_iota(jnp.int32, (128, 128), 1)
        earlier = jnp.where((r128 < TOK) & (r128 < lax.rem(l128, TOK)), 1.0, 0.0).astype(BF16)
        for t in range(TICKS):
            ids, prob = ids_ref[t], prob_ref[t]
            gate = prob / jnp.sum(prob, axis=0, keepdims=True)
            member = jnp.zeros((SIDE * SIDE, 128), F32)
            gates = jnp.zeros((SIDE * SIDE, 128), F32)
            for k in range(TOPK):
                hit = named == ids[k : k + 1, :]
                member = member + jnp.where(hit, 1.0, 0.0)
                gates = gates + jnp.where(hit, gate[k : k + 1, :], 0.0)
            slots = jnp.where(member > 0.5, dot(member.astype(BF16), earlier), -1.0)
            ms[:, 16 * t : 16 * t + 8, :] = slots.reshape(SIDE, SIDE, 128)
            ms[:, 16 * t + 8 : 16 * t + 16, :] = gates.reshape(SIDE, SIDE, 128)
        mr[0] = ms[0]

    def build_maps(t):
        row = lax.broadcasted_iota(jnp.int32, (128, 128), 0)
        lane = lax.broadcasted_iota(jnp.int32, (128, 128), 1)
        same = (lax.rem(row, 16) // 8) == (lane // TOK)
        slot = lax.rem(row, 8).astype(F32)
        xrow = lax.broadcasted_iota(jnp.int32, (64, 128), 0)
        xlane = lax.broadcasted_iota(jnp.int32, (64, 128), 1)
        low = lax.broadcasted_iota(jnp.int32, (8, 128), 1) < TOK
        for q in range(4):
            slots = jnp.where(low, mr[2 * q, 16 * t : 16 * t + 8, :], mr[2 * q + 1, 16 * t : 16 * t + 8, :])
            gates = jnp.where(low, mr[2 * q, 16 * t + 8 : 16 * t + 16, :], mr[2 * q + 1, 16 * t + 8 : 16 * t + 16, :])
            wide = jnp.concatenate([jnp.broadcast_to(slots[i : i + 1], (16, 128)) for i in range(8)], axis=0)
            wide_gate = jnp.concatenate([jnp.broadcast_to(gates[i : i + 1], (16, 128)) for i in range(8)], axis=0)
            hit = same & (wide == slot)
            omat[t, q] = jnp.where(hit, 1.0, 0.0).astype(BF16)
            got[t, q] = jnp.where(hit, wide_gate, 0.0).T.astype(BF16)
            wide = jnp.concatenate([jnp.broadcast_to(slots[i : i + 1], (8, 128)) for i in range(8)], axis=0)
            wide_gate = jnp.concatenate([jnp.broadcast_to(gates[i : i + 1], (8, 128)) for i in range(8)], axis=0)
            hit = (lax.rem(xrow, 8) == 2 * q + xlane // TOK) & (wide == 8.0)
            o8[t, :, 128 * q : 128 * q + 128] = jnp.where(hit, 1.0, 0.0).astype(BF16)
            spread_gate = jnp.concatenate([jnp.where(hit, wide_gate, 0.0), jnp.zeros((64, 128), F32)], axis=0)
            g8t[t, q] = spread_gate.T.astype(BF16)

    def pack_extra(rows, ref):
        for p in range(SIDE):
            part = rows[8 * p : 8 * p + 8]
            ref[p] = jnp.concatenate([part[:, :C2], part[:, C2:]], axis=0).astype(BF16)

    def unpack_extra(ref):
        parts = []
        for p in range(SIDE):
            part = ref[p].astype(F32)
            parts.append(jnp.concatenate([part[:8], part[8:]], axis=1))
        return jnp.concatenate(parts, axis=0).astype(BF16)

    x0 = x_ref[...].astype(F32)
    put_squares(0, x0)
    make_meta()
    greeted = 2 * (SIDE - 1) + 1 + jnp.where(pipe > 0, 1, 0) + jnp.where(pipe < lax.axis_size("pipe") - 1, 1, 0)
    pl.semaphore_wait(barrier, greeted)
    squares_copy(0).start()
    for j in range(1, SIDE):
        remote(ms.at[j], mr.at[POS[j]], meta_sem.at[0], meta_sem.at[1], first(j)).start()
    xn[...] = x_ref[...]

    for t in range(TICKS):
        if t > 0:
            put_squares(t, xn[...].astype(F32))
            squares_copy(t).start()
        squares_copy(t).wait()
        scale = lax.rsqrt((sqs[t] + sqr[t]) / (2.0 * D) + EPS)[:, :1]

        def ring_copy(k, j):
            parent = PARENT[j]
            return remote(
                gb.at[t, k, pl.ds(POS[parent] * TOK, TOK)], gb.at[t, k, pl.ds(POS[j] * TOK, TOK)],
                ring_send.at[t, k], ring_recv.at[t, k, j], first(j - parent),
            )

        for k in range(NC):
            cols = slice(k * C, k * C + C)
            gb[t, k, :TOK] = (xn[:, cols].astype(F32) * scale * gain_ref[:, cols]).astype(BF16)
            for j in CHILDREN[0]:
                ring_copy(k, j).start()
        if t == 0:
            remote(mr.at[pl.ds(1, 7)], mr.at[pl.ds(1, 7)], meta_sem.at[0], meta_sem.at[1], first(1)).wait_recv()
        build_maps(t)

        for step in range(4):
            for k in range(NC):
                for j in ARRIVALS[step]:
                    ring_copy(k, j).wait_recv()
                    for child in CHILDREN[j]:
                        ring_copy(k, child).start()
            q = step
            for k in range(NC):
                picked = dot(omat[t, q], gb[t, k, 128 * q : 128 * q + 128, :]).astype(BF16).reshape(SIDE, 16, C)
                mb[t, k, q] = picked
                rb[t, k, 0, q] = picked[0]
                for i in range(1, SIDE):
                    p = POS[i]
                    remote(mb.at[t, k, q, p], rb.at[t, k, p, q], main_sem.at[t, k, 0], main_sem.at[t, k, 1], second(i)).start()
                if step == 3:
                    pack_extra(dot(o8[t], gb[t, k]), xb.at[t, k])
                    rxb[t, k, 0] = xb[t, k, 0]
                    for i in range(1, SIDE):
                        p = POS[i]
                        remote(xb.at[t, k, p], rxb.at[t, k, p], ext_sem.at[t, k, 0], ext_sem.at[t, k, 1], second(i)).start()

        if t == 0:
            up_copy.wait()
        for k in range(NC):
            remote(rb.at[t, k, pl.ds(1, 7)], rb.at[t, k, pl.ds(1, 7)], main_sem.at[t, k, 0], main_sem.at[t, k, 1], second(1)).wait_recv()
            remote(rxb.at[t, k, pl.ds(1, 7)], rxb.at[t, k, pl.ds(1, 7)], ext_sem.at[t, k, 0], ext_sem.at[t, k, 1], second(1)).wait_recv()
            rows = rb[t, k].reshape(512, C)
            extra = unpack_extra(rxb.at[t, k])
            for h in range(HC):
                hs = slice(h * HW, h * HW + HW)
                weight = wup[k * C : k * C + C, hs]
                main_part, extra_part = dot(rows, weight), dot(extra, weight)
                if k > 0:
                    main_part = main_part + pacc[:512, hs]
                    extra_part = extra_part + pacc[512:, hs]
                if k < NC - 1:
                    pacc[:512, hs] = main_part
                    pacc[512:, hs] = extra_part
                else:
                    ps[t, h, :512] = main_part.astype(BF16)
                    ps[t, h, 512:] = extra_part.astype(BF16)
                    remote(ps.at[t, h], pr.at[t, h], p_sem.at[t, h, 0], p_sem.at[t, h, 1], other_core).start()
        xrow = lax.broadcasted_iota(jnp.int32, (64, 64), 0)
        xlane = lax.broadcasted_iota(jnp.int32, (64, 64), 1)
        swap = jnp.where(xlane == lax.rem(xrow, 8) * 8 + xrow // 8, 1.0, 0.0).astype(BF16)
        for h in range(HC):
            remote(ps.at[t, h], pr.at[t, h], p_sem.at[t, h, 0], p_sem.at[t, h, 1], other_core).wait_recv()
            theirs = pr[t, h, :512].astype(F32).reshape(SIDE, SIDE, 8, HW)
            for p in range(SIDE):
                total = ps[t, h, 64 * p : 64 * p + 64].astype(F32) + theirs[:, p].reshape(64, HW)
                hid[64 * p : 64 * p + 64, h * HW : h * HW + HW] = (total / (1.0 + jnp.exp(-total))).astype(BF16)
            total = ps[t, h, 512:].astype(F32) + dot(swap, pr[t, h, 512:])
            hid[512:, h * HW : h * HW + HW] = (total / (1.0 + jnp.exp(-total))).astype(BF16)
        if t == 0:
            down_copy.wait()

        for k in range(NC):
            weight = wdn[:, k * C : k * C + C]
            made = dot(hid[:512], weight).astype(BF16).reshape(SIDE, 4, 16, C)
            ob[t, k] = made
            for q in range(4):
                tb[t, k, q, 0] = made[0, q]
            pack_extra(dot(hid[512:], weight), oxb.at[t, k])
            txb[t, k, 0] = oxb[t, k, 0]
            for i in range(1, SIDE):
                p = POS[i]
                remote(ob.at[t, k, p], tb.at[t, k, :, p], rmain_sem.at[t, k, 0], rmain_sem.at[t, k, 1], second(-i)).start()
                remote(oxb.at[t, k, p], txb.at[t, k, p], rext_sem.at[t, k, 0], rext_sem.at[t, k, 1], second(-i)).start()

        def back_copy(k, j):
            return remote(
                sb.at[t, k, j], rr.at[t, k, j], back_send.at[t, k], back_recv.at[t, k, j], first(PARENT[j] - j),
            )

        for q in (3, 2, 1, 0):
            for k in range(NC):
                if q == 3:
                    remote(rb.at[t, k, pl.ds(1, 7)], rb.at[t, k, pl.ds(1, 7)], rmain_sem.at[t, k, 0], rmain_sem.at[t, k, 1], second(1)).wait_recv()
                    remote(txb.at[t, k, pl.ds(1, 7)], txb.at[t, k, pl.ds(1, 7)], rext_sem.at[t, k, 0], rext_sem.at[t, k, 1], second(1)).wait_recv()
                part = dot(got[t, q], tb[t, k, q].reshape(128, C))
                part = part + dot(g8t[t, q][:, :64], unpack_extra(txb.at[t, k]))
                for h in (1, 0):
                    j = OFFSETS[2 * q + h]
                    total = part[64 * h : 64 * h + 64]
                    for child in CHILDREN[j]:
                        back_copy(k, child).wait_recv()
                        total = total + rr[t, k, child].astype(F32)
                    if j > 0:
                        sb[t, k, j] = total.astype(BF16)
                        back_copy(k, j).start()
                    else:
                        cols = slice(k * C, k * C + C)
                        y = (xn[:, cols].astype(F32) + total).astype(BF16)
                        if t == TICKS - 1:
                            out_ref[:, cols] = y
                        else:
                            shs[t, k] = y

                            @pl.when(pipe < lax.axis_size("pipe") - 1)
                            def _():
                                remote(shs.at[t, k], shr.at[t, k], sh_send.at[t, k], sh_recv.at[t, k], {"pipe": pipe + 1}).start()

        if t < TICKS - 1:
            @pl.when(pipe > 0)
            def _():
                for k in range(NC):
                    remote(shs.at[t, k], shr.at[t, k], sh_send.at[t, k], sh_recv.at[t, k], {"pipe": pipe - 1}).wait_recv()
                    xn[:, k * C : k * C + C] = shr[t, k]

            @pl.when(pipe == 0)
            def _():
                xn[...] = fresh_ref[t]

    remote(mr.at[pl.ds(1, 7)], mr.at[pl.ds(1, 7)], meta_sem.at[0], meta_sem.at[1], first(1)).wait_send()
    for t in range(TICKS):
        for k in range(NC):
            seven = pl.ds(1, 7)
            remote(gb.at[t, k, pl.ds(64, 448)], gb.at[t, k, pl.ds(64, 448)], ring_send.at[t, k], ring_recv.at[t, k, 0], first(1)).wait_send()
            remote(rb.at[t, k, seven], rb.at[t, k, seven], main_sem.at[t, k, 0], main_sem.at[t, k, 1], second(1)).wait_send()
            remote(rxb.at[t, k, seven], rxb.at[t, k, seven], ext_sem.at[t, k, 0], ext_sem.at[t, k, 1], second(1)).wait_send()
            remote(rb.at[t, k, seven], rb.at[t, k, seven], rmain_sem.at[t, k, 0], rmain_sem.at[t, k, 1], second(1)).wait_send()
            remote(txb.at[t, k, seven], txb.at[t, k, seven], rext_sem.at[t, k, 0], rext_sem.at[t, k, 1], second(1)).wait_send()
            remote(sb.at[t, k, seven], sb.at[t, k, seven], back_send.at[t, k], back_recv.at[t, k, 0], first(1)).wait_send()
        for h in range(HC):
            remote(ps.at[t, h], pr.at[t, h], p_sem.at[t, h, 0], p_sem.at[t, h, 1], other_core).wait_send()

    @pl.when(pipe < lax.axis_size("pipe") - 1)
    def _():
        for t in range(TICKS - 1):
            for k in range(NC):
                remote(shs.at[t, k], shr.at[t, k], sh_send.at[t, k], sh_recv.at[t, k], {"pipe": pipe + 1}).wait_send()


def on_device(in_flight, fresh_batch, norm_gain, up_weight, down_weight, expert_ids, route_prob):
    ids = jnp.swapaxes(expert_ids[:, 0], 1, 2)
    ids = jnp.concatenate([ids, ids], axis=2)
    prob = jnp.swapaxes(route_prob[:, 0], 1, 2)
    prob = jnp.concatenate([prob, prob], axis=2)
    vmem = pl.BlockSpec(memory_space=pltpu.VMEM)
    hbm = pl.BlockSpec(memory_space=pl.ANY)
    dma = pltpu.SemaphoreType.DMA
    scratch = [
        pltpu.VMEM((D, HID), BF16), pltpu.VMEM((HID, D), BF16),
        pltpu.VMEM((TICKS, NC, 512, C), BF16),
        pltpu.VMEM((TICKS, NC, 4, SIDE, 16, C), BF16),
        pltpu.VMEM((TICKS, NC, SIDE, 16, C2), BF16),
        pltpu.VMEM((TICKS, NC, SIDE, 4, 16, C), BF16),
        pltpu.VMEM((TICKS, NC, SIDE, 16, C2), BF16),
        pltpu.VMEM((576, HID), F32),
        pltpu.VMEM((TICKS, HC, 576, HW), BF16),
        pltpu.VMEM((TICKS, HC, 576, HW), BF16),
        pltpu.VMEM((576, HID), BF16),
        pltpu.VMEM((TICKS, NC, SIDE, 4, 16, C), BF16),
        pltpu.VMEM((TICKS, NC, SIDE, 16, C2), BF16),
        pltpu.VMEM((TICKS, NC, 4, SIDE, 16, C), BF16),
        pltpu.VMEM((TICKS, NC, SIDE, 16, C2), BF16),
        pltpu.VMEM((TICKS, NC, SIDE, TOK, C), BF16),
        pltpu.VMEM((TICKS, NC, SIDE, TOK, C), BF16),
        pltpu.VMEM((TICKS, TOK, 128), F32),
        pltpu.VMEM((TICKS, TOK, 128), F32),
        pltpu.VMEM((TICKS, NC, TOK, C), BF16),
        pltpu.VMEM((TICKS, NC, TOK, C), BF16),
        pltpu.VMEM((TOK, D), BF16),
        pltpu.VMEM((SIDE, 32, 128), F32),
        pltpu.VMEM((SIDE, 32, 128), F32),
        pltpu.VMEM((TICKS, 4, 128, 128), BF16),
        pltpu.VMEM((TICKS, 64, 512), BF16),
        pltpu.VMEM((TICKS, 4, 128, 128), BF16),
        pltpu.VMEM((TICKS, 4, 128, 128), BF16),
        dma((2,)), dma((2,)), dma((TICKS, 2)), dma((TICKS, NC)), dma((TICKS, NC)),
        dma((TICKS, NC)), dma((TICKS, NC, SIDE)), dma((TICKS, NC, 2)), dma((TICKS, NC, 2)),
        dma((TICKS, HC, 2)), dma((TICKS, NC, 2)), dma((TICKS, NC, 2)),
        dma((TICKS, NC)), dma((TICKS, NC, SIDE)),
    ]
    y = pl.pallas_call(
        kernel,
        name="window",
        out_shape=jax.ShapeDtypeStruct((TOK, D), BF16),
        in_specs=[vmem, vmem, vmem, hbm, hbm, vmem, vmem],
        out_specs=vmem,
        scratch_shapes=scratch,
        compiler_params=pltpu.CompilerParams(
            collective_id=0, has_side_effects=True, vmem_limit_bytes=48 * 2**20
        ),
    )(in_flight[0], fresh_batch, norm_gain, up_weight[0, 0], down_weight[0, 0], ids, prob)
    return y[None]


def solution(mesh):
    placed = (
        P("pipe", "expert", "tensor"),
        P(None, "expert", "tensor"),
        P("pipe", "tensor"),
        P("pipe", "expert", "tensor", None),
        P("pipe", "expert", None, "tensor"),
        P(None, "pipe", "expert", None),
        P(None, "pipe", "expert", None),
    )
    return jax.shard_map(
        on_device,
        mesh=mesh,
        in_specs=placed,
        out_specs=P("pipe", "expert", "tensor"),
        check_vma=False,
    )
```

time: 427 us -> 164 us (0.38)
  waiting for transfers between devices: 183 us -> 0 us
  Pallas kernels: 0 us -> 156 us
  blocking collectives: 144 us -> 0 us
  local copies, waits for them, and re-layouts: 37.1 us -> 5.97 us
  starting transfers between devices: 30.1 us -> 0 us
  between operations: 13.7 us -> 0.02 us
  matrix products: 11.4 us -> 0 us
  other arithmetic: 6.76 us -> 1.69 us
    pallas_call x0 -> x1, Pallas kernels: none -> 156 us  [on_device(): pl.pallas_call(kernel, name='window', out_shape=jax.ShapeDtypeStruct((TOK...]
    all_to_all x2 -> x0, blocking collectives: 139 us -> none  [run_section(): lax.all_to_all(outgoing, 'expert', split_axis=0, concat_axis=0, tiled=True)]
    all_to_all x2 -> x0, waiting for transfers between devices: 101 us -> none  [run_section(): lax.all_to_all(produced, 'expert', split_axis=0, concat_axis=0, tiled=True)]
    psum x2 -> x0, waiting for transfers between devices: 76.1 us -> none  [run_section(): lax.psum(partial_up.astype(jnp.bfloat16), 'tensor').astype(jnp.float32)]
    all_to_all x2 -> x0, starting transfers between devices: 28.8 us -> none  [run_section(): lax.all_to_all(produced, 'expert', split_axis=0, concat_axis=0, tiled=True)]
    gather x8 -> x0, local copies, waits for them, and re-layouts: 13.5 us -> none  [the longest x6 7.88 us: slot_table(): position = jnp.take_along_axis(earlier, block_ids, axis=1)]
    dot_general x4 -> x0, matrix products: 11.4 us -> none  [the longest x2 6.86 us: run_section(): jnp.einsum('erd,edh->erh', expert_rows, up_local, preferred_element_type=...]
    reshape x6 -> x0, local copies, waits for them, and re-layouts: 8.47 us -> none  [the longest x2 5.08 us: run_section(): picked = returned.reshape(experts_all * capacity, half_width)[slot_index]]
  transfers between devices with their start and end apart: 5 -> 0, of which waited for: 5 -> 0; matrix products, arithmetic and copies ran while one was open for 1% -> 0% of each run, Pallas kernels for 0% -> 0%
where the time goes in v1:
time: 164 us; the launch traced here: 163 us
  Pallas kernels  156 us (95%)
  local copies, waits for them, and re-layouts  5.97 us (4%)
  other arithmetic  1.69 us (1%)
    pallas_call x1, Pallas kernels, on_device(): pl.pallas_call(kernel, name='window', out_shape=jax.ShapeDtypeStruct((TOK...  156 us
    unnamed x11, local copies, waits for them, and re-layouts  5.97 us

profile of v1, /device:TPU:14, one launch (start us, length us, event | category | flops | bytes accessed | tf_op | source)
XLA Modules:
  0.0 163.4 jit_solution(2857209168047966581)
XLA Ops:
  0.0 0.8 pad_add_fusion.ids_ref
  0.8 0.8 pad_maximum_fusion.prob_ref
  1.7 0.0 copy-start
  1.7 1.4 copy-done
  3.1 0.0 copy-start.1
  3.1 1.4 copy-done.1
  4.5 0.0 copy-start.2
  4.5 0.9 copy-done.2
  5.4 0.0 copy-start.3
  5.4 0.9 copy-done.3
  6.3 0.0 copy-start.4
  6.3 0.7 copy-done.4
  7.0 155.7 %window.1 = bf16[64,1024]{1,0:T(8,128)(2,1)S(1)} custom-call(bf16[64,1024]{1,0:T(8,128)(2,1)S(1)} %bitcast.13, bf16[1,64,1024]{2,1,0:T(8,128)(2,1)S(1)} %copy-done.3, f32[1,1024]{1,0:T(1,128)S(1)} %copy-done.4, bf16[1024,768]{1,0:T(8,128)(2,1)S(1)} %bitcast.10, bf16[768,1024]{1,0:T(8,128)(2,1)S(1)} %bitcast.11, s32[2,8,128]{2,1,0:T(8,128)S(1)} %pad_add_fusion.ids_ref, ...), custom_call_target="tpu_custom_call" | custom-call | tf_op jit(solution)/shard_map/window/pallas_call | solution.py:367
  162.7 0.7 copy.9
Async XLA Ops:
  1.7 1.4 copy-start
  3.1 1.4 copy-start.1
  4.5 0.9 copy-start.2
  5.4 0.9 copy-start.3
  6.3 0.7 copy-start.4

commit v2 on v1

--- a/solution.py
+++ b/solution.py
@@ -16,8 +16,6 @@
 TOPK = 8
 D = 1024
 HID = 768
-HC = 3
-HW = HID // HC
 NC = 2
 C = D // NC
 C2 = C // 2
@@ -28,6 +26,7 @@
 PARENT = {1: 0, 2: 1, 3: 2, 4: 3, 7: 0, 6: 7, 5: 6}
 CHILDREN = {j: tuple(c for c in PARENT if PARENT[c] == j) for j in range(SIDE)}
 ARRIVALS = ((1, 7), (2, 6), (3, 5), (4,))
+FAR_FIRST = (4, 3, 5, 2, 6, 1, 7)
 
 
 def offset_of(position):
@@ -40,11 +39,12 @@
 
 
 def kernel(
-    x_ref, fresh_ref, gain_ref, up_hbm, down_hbm, ids_ref, prob_ref, out_ref,
-    wup, wdn, gb, mb, xb, rb, rxb, pacc, ps, pr, hid, ob, oxb, tb, txb, sb, rr,
-    sqs, sqr, shs, shr, xn, ms, mr, omat, o8, got, g8t,
-    wsem, meta_sem, sq_sem, sh_send, sh_recv, ring_send, ring_recv, main_sem, ext_sem,
-    p_sem, rmain_sem, rext_sem, back_send, back_recv,
+    x_hbm, fresh_hbm, gain_hbm, up_hbm, down_hbm, ids_hbm, prob_hbm, out_ref,
+    xn, fresh_ref, gain_ref, wup, wdn, ids_ref, prob_ref,
+    gb, mb, xb, rb, rxb, ps, pr, pse, pre, ob, oxb, tb, txb, te, sb, rr,
+    sqs, sqr, shs, shr, ms, mr, omat, o8, got, g8t,
+    load_sem, meta_sem, sq_sem, sh_send, sh_recv, ring_send, ring_recv, main_send, main_recv, ext_sem,
+    p_sem, pe_sem, rmain_send, rmain_recv, rext_sem, back_send, back_recv,
 ):
     core = lax.axis_index("tensor")
     expert = lax.axis_index("expert")
@@ -69,10 +69,16 @@
             device_id=device, device_id_type=MESH,
         )
 
-    up_copy = pltpu.make_async_copy(up_hbm, wup, wsem.at[0])
-    down_copy = pltpu.make_async_copy(down_hbm, wdn, wsem.at[1])
-    up_copy.start()
-    down_copy.start()
+    loads = [
+        pltpu.make_async_copy(source, held, load_sem.at[n])
+        for n, (source, held) in enumerate((
+            (x_hbm, xn), (ids_hbm, ids_ref), (prob_hbm, prob_ref), (gain_hbm, gain_ref),
+            (fresh_hbm, fresh_ref), (up_hbm, wup), (down_hbm, wdn),
+        ))
+    ]
+    for load in loads:
+        load.start()
+    x_load, ids_load, prob_load, gain_load, fresh_load, up_load, down_load = loads
 
     barrier = pltpu.get_barrier_semaphore()
     other_core = {"tensor": 1 - core}
@@ -109,7 +115,8 @@
         l128 = lax.broadcasted_iota(jnp.int32, (128, 128), 1)
         earlier = jnp.where((r128 < TOK) & (r128 < lax.rem(l128, TOK)), 1.0, 0.0).astype(BF16)
         for t in range(TICKS):
-            ids, prob = ids_ref[t], prob_ref[t]
+            ids = jnp.concatenate([ids_ref[t], ids_ref[t]], axis=1)
+            prob = jnp.concatenate([prob_ref[t], prob_ref[t]], axis=1)
             gate = prob / jnp.sum(prob, axis=0, keepdims=True)
             member = jnp.zeros((SIDE * SIDE, 128), F32)
             gates = jnp.zeros((SIDE * SIDE, 128), F32)
@@ -157,15 +164,17 @@
             parts.append(jnp.concatenate([part[:8], part[8:]], axis=1))
         return jnp.concatenate(parts, axis=0).astype(BF16)
 
-    x0 = x_ref[...].astype(F32)
-    put_squares(0, x0)
+    x_load.wait()
+    put_squares(0, xn[...].astype(F32))
+    ids_load.wait()
+    prob_load.wait()
     make_meta()
     greeted = 2 * (SIDE - 1) + 1 + jnp.where(pipe > 0, 1, 0) + jnp.where(pipe < lax.axis_size("pipe") - 1, 1, 0)
     pl.semaphore_wait(barrier, greeted)
     squares_copy(0).start()
     for j in range(1, SIDE):
         remote(ms.at[j], mr.at[POS[j]], meta_sem.at[0], meta_sem.at[1], first(j)).start()
-    xn[...] = x_ref[...]
+    gain_load.wait()
 
     for t in range(TICKS):
         if t > 0:
@@ -188,7 +197,39 @@
                 ring_copy(k, j).start()
         if t == 0:
             remote(mr.at[pl.ds(1, 7)], mr.at[pl.ds(1, 7)], meta_sem.at[0], meta_sem.at[1], first(1)).wait_recv()
-        build_maps(t)
+            build_maps(t)
+
+        def main_copy(k, q, i):
+            p = POS[i]
+            return remote(mb.at[t, k, q, p], rb.at[t, k, q, p], main_send.at[t, k], main_recv.at[t, k, q], second(i))
+
+        def products_copy(q):
+            return remote(ps.at[t, q], pr.at[t, q], p_sem.at[t, q, 0], p_sem.at[t, q, 1], other_core)
+
+        def extra_products_copy():
+            return remote(pse.at[t], pre.at[t], pe_sem.at[t, 0], pe_sem.at[t, 1], other_core)
+
+        def up_rows(q):
+            if t == 0 and q == 0:
+                up_load.wait()
+            total = None
+            for k in range(NC):
+                seven = rb.at[t, k, q, pl.ds(1, 7)]
+                remote(seven, seven, main_send.at[t, k], main_recv.at[t, k, q], second(1)).wait_recv()
+                part = dot(rb[t, k, q].reshape(128, C), wup[k * C : k * C + C])
+                total = part if total is None else total + part
+            ps[t, q] = total.astype(BF16)
+            products_copy(q).start()
+
+        def up_extra():
+            total = None
+            for k in range(NC):
+                seven = rxb.at[t, k, pl.ds(1, 7)]
+                remote(seven, seven, ext_sem.at[t, k, 0], ext_sem.at[t, k, 1], second(1)).wait_recv()
+                part = dot(unpack_extra(rxb.at[t, k]), wup[k * C : k * C + C])
+                total = part if total is None else total + part
+            pse[t] = total.astype(BF16)
+            extra_products_copy().start()
 
         for step in range(4):
             for k in range(NC):
@@ -200,77 +241,74 @@
             for k in range(NC):
                 picked = dot(omat[t, q], gb[t, k, 128 * q : 128 * q + 128, :]).astype(BF16).reshape(SIDE, 16, C)
                 mb[t, k, q] = picked
-                rb[t, k, 0, q] = picked[0]
-                for i in range(1, SIDE):
-                    p = POS[i]
-                    remote(mb.at[t, k, q, p], rb.at[t, k, p, q], main_sem.at[t, k, 0], main_sem.at[t, k, 1], second(i)).start()
+                rb[t, k, q, 0] = picked[0]
+                for i in FAR_FIRST:
+                    main_copy(k, q, i).start()
                 if step == 3:
                     pack_extra(dot(o8[t], gb[t, k]), xb.at[t, k])
                     rxb[t, k, 0] = xb[t, k, 0]
-                    for i in range(1, SIDE):
+                    for i in FAR_FIRST:
                         p = POS[i]
                         remote(xb.at[t, k, p], rxb.at[t, k, p], ext_sem.at[t, k, 0], ext_sem.at[t, k, 1], second(i)).start()
-
+            if step >= 2:
+                up_rows(step - 2)
         if t == 0:
-            up_copy.wait()
-        for k in range(NC):
-            remote(rb.at[t, k, pl.ds(1, 7)], rb.at[t, k, pl.ds(1, 7)], main_sem.at[t, k, 0], main_sem.at[t, k, 1], second(1)).wait_recv()
-            remote(rxb.at[t, k, pl.ds(1, 7)], rxb.at[t, k, pl.ds(1, 7)], ext_sem.at[t, k, 0], ext_sem.at[t, k, 1], second(1)).wait_recv()
-            rows = rb[t, k].reshape(512, C)
-            extra = unpack_extra(rxb.at[t, k])
-            for h in range(HC):
-                hs = slice(h * HW, h * HW + HW)
-                weight = wup[k * C : k * C + C, hs]
-                main_part, extra_part = dot(rows, weight), dot(extra, weight)
-                if k > 0:
-                    main_part = main_part + pacc[:512, hs]
-                    extra_part = extra_part + pacc[512:, hs]
-                if k < NC - 1:
-                    pacc[:512, hs] = main_part
-                    pacc[512:, hs] = extra_part
-                else:
-                    ps[t, h, :512] = main_part.astype(BF16)
-                    ps[t, h, 512:] = extra_part.astype(BF16)
-                    remote(ps.at[t, h], pr.at[t, h], p_sem.at[t, h, 0], p_sem.at[t, h, 1], other_core).start()
+            for later in range(1, TICKS):
+                build_maps(later)
+        up_rows(2)
+        up_rows(3)
+        up_extra()
+
         xrow = lax.broadcasted_iota(jnp.int32, (64, 64), 0)
         xlane = lax.broadcasted_iota(jnp.int32, (64, 64), 1)
         swap = jnp.where(xlane == lax.rem(xrow, 8) * 8 + xrow // 8, 1.0, 0.0).astype(BF16)
-        for h in range(HC):
-            remote(ps.at[t, h], pr.at[t, h], p_sem.at[t, h, 0], p_sem.at[t, h, 1], other_core).wait_recv()
-            theirs = pr[t, h, :512].astype(F32).reshape(SIDE, SIDE, 8, HW)
-            for p in range(SIDE):
-                total = ps[t, h, 64 * p : 64 * p + 64].astype(F32) + theirs[:, p].reshape(64, HW)
-                hid[64 * p : 64 * p + 64, h * HW : h * HW + HW] = (total / (1.0 + jnp.exp(-total))).astype(BF16)
-            total = ps[t, h, 512:].astype(F32) + dot(swap, pr[t, h, 512:])
-            hid[512:, h * HW : h * HW + HW] = (total / (1.0 + jnp.exp(-total))).astype(BF16)
+        for q in range(4):
+            products_copy(q).wait_recv()
+        extra_products_copy().wait_recv()
         if t == 0:
-            down_copy.wait()
-
-        for k in range(NC):
-            weight = wdn[:, k * C : k * C + C]
-            made = dot(hid[:512], weight).astype(BF16).reshape(SIDE, 4, 16, C)
-            ob[t, k] = made
-            for q in range(4):
-                tb[t, k, q, 0] = made[0, q]
-            pack_extra(dot(hid[512:], weight), oxb.at[t, k])
-            txb[t, k, 0] = oxb[t, k, 0]
-            for i in range(1, SIDE):
-                p = POS[i]
-                remote(ob.at[t, k, p], tb.at[t, k, :, p], rmain_sem.at[t, k, 0], rmain_sem.at[t, k, 1], second(-i)).start()
-                remote(oxb.at[t, k, p], txb.at[t, k, p], rext_sem.at[t, k, 0], rext_sem.at[t, k, 1], second(-i)).start()
+            down_load.wait()
+
+        def down_extra():
+            total = pse[t].astype(F32) + dot(swap, pre[t])
+            hidden = (total / (1.0 + jnp.exp(-total))).astype(BF16)
+            made = dot(hidden, wdn[...])
+            for k in range(NC):
+                pack_extra(made[:, k * C : k * C + C], oxb.at[t, k])
+                txb[t, k, 0] = oxb[t, k, 0]
+                for i in FAR_FIRST:
+                    p = POS[i]
+                    remote(oxb.at[t, k, p], txb.at[t, k, p], rext_sem.at[t, k, 0], rext_sem.at[t, k, 1], second(-i)).start()
+
+        def down_rows(q):
+            parts = []
+            for n in range(4):
+                block = pr[t, n, 32 * q : 32 * q + 32].astype(F32)
+                parts += [block[:8], block[16:24], block[8:16], block[24:]]
+            total = ps[t, q].astype(F32) + jnp.concatenate(parts, axis=0)
+            hidden = (total / (1.0 + jnp.exp(-total))).astype(BF16)
+            for k in range(NC):
+                made = dot(hidden, wdn[:, k * C : k * C + C]).astype(BF16).reshape(SIDE, 16, C)
+                ob[t, k, q] = made
+                tb[t, k, q, 0] = made[0]
+                for i in FAR_FIRST:
+                    p = POS[i]
+                    remote(ob.at[t, k, q, p], tb.at[t, k, q, p], rmain_send.at[t, k], rmain_recv.at[t, k, q], second(-i)).start()
 
         def back_copy(k, j):
             return remote(
                 sb.at[t, k, j], rr.at[t, k, j], back_send.at[t, k], back_recv.at[t, k, j], first(PARENT[j] - j),
             )
 
-        for q in (3, 2, 1, 0):
+        def sum_pair(q):
             for k in range(NC):
                 if q == 3:
-                    remote(rb.at[t, k, pl.ds(1, 7)], rb.at[t, k, pl.ds(1, 7)], rmain_sem.at[t, k, 0], rmain_sem.at[t, k, 1], second(1)).wait_recv()
-                    remote(txb.at[t, k, pl.ds(1, 7)], txb.at[t, k, pl.ds(1, 7)], rext_sem.at[t, k, 0], rext_sem.at[t, k, 1], second(1)).wait_recv()
+                    seven = txb.at[t, k, pl.ds(1, 7)]
+                    remote(seven, seven, rext_sem.at[t, k, 0], rext_sem.at[t, k, 1], second(1)).wait_recv()
+                    te[k] = unpack_extra(txb.at[t, k])
+                seven = tb.at[t, k, q, pl.ds(1, 7)]
+                remote(seven, seven, rmain_send.at[t, k], rmain_recv.at[t, k, q], second(1)).wait_recv()
                 part = dot(got[t, q], tb[t, k, q].reshape(128, C))
-                part = part + dot(g8t[t, q][:, :64], unpack_extra(txb.at[t, k]))
+                part = part + dot(g8t[t, q][:, :64], te[k])
                 for h in (1, 0):
                     j = OFFSETS[2 * q + h]
                     total = part[64 * h : 64 * h + 64]
@@ -292,7 +330,20 @@
                             def _():
                                 remote(shs.at[t, k], shr.at[t, k], sh_send.at[t, k], sh_recv.at[t, k], {"pipe": pipe + 1}).start()
 
+        down_extra()
+        down_rows(3)
+        down_rows(2)
+        sum_pair(3)
+        down_rows(1)
+        sum_pair(2)
+        down_rows(0)
+        sum_pair(1)
+        sum_pair(0)
+
         if t < TICKS - 1:
+            if t == 0:
+                fresh_load.wait()
+
             @pl.when(pipe > 0)
             def _():
                 for k in range(NC):
@@ -303,18 +354,26 @@
             def _():
                 xn[...] = fresh_ref[t]
 
-    remote(mr.at[pl.ds(1, 7)], mr.at[pl.ds(1, 7)], meta_sem.at[0], meta_sem.at[1], first(1)).wait_send()
+    seven = pl.ds(1, 7)
+
+    def sent(ref, semaphore):
+        pltpu.make_async_remote_copy(
+            src_ref=ref, dst_ref=ref, send_sem=semaphore, recv_sem=meta_sem.at[1],
+            device_id=other_core, device_id_type=MESH,
+        ).wait_send()
+
+    sent(mr.at[seven], meta_sem.at[0])
     for t in range(TICKS):
         for k in range(NC):
-            seven = pl.ds(1, 7)
-            remote(gb.at[t, k, pl.ds(64, 448)], gb.at[t, k, pl.ds(64, 448)], ring_send.at[t, k], ring_recv.at[t, k, 0], first(1)).wait_send()
-            remote(rb.at[t, k, seven], rb.at[t, k, seven], main_sem.at[t, k, 0], main_sem.at[t, k, 1], second(1)).wait_send()
-            remote(rxb.at[t, k, seven], rxb.at[t, k, seven], ext_sem.at[t, k, 0], ext_sem.at[t, k, 1], second(1)).wait_send()
-            remote(rb.at[t, k, seven], rb.at[t, k, seven], rmain_sem.at[t, k, 0], rmain_sem.at[t, k, 1], second(1)).wait_send()
-            remote(txb.at[t, k, seven], txb.at[t, k, seven], rext_sem.at[t, k, 0], rext_sem.at[t, k, 1], second(1)).wait_send()
-            remote(sb.at[t, k, seven], sb.at[t, k, seven], back_send.at[t, k], back_recv.at[t, k, 0], first(1)).wait_send()
-        for h in range(HC):
-            remote(ps.at[t, h], pr.at[t, h], p_sem.at[t, h, 0], p_sem.at[t, h, 1], other_core).wait_send()
+            sent(gb.at[t, k, pl.ds(64, 448)], ring_send.at[t, k])
+            sent(mb.at[t, k, :, seven], main_send.at[t, k])
+            sent(xb.at[t, k, seven], ext_sem.at[t, k, 0])
+            sent(ob.at[t, k, :, seven], rmain_send.at[t, k])
+            sent(oxb.at[t, k, seven], rext_sem.at[t, k, 0])
+            sent(sb.at[t, k, seven], back_send.at[t, k])
+        for q in range(4):
+            sent(ps.at[t, q], p_sem.at[t, q, 0])
+        sent(pse.at[t], pe_sem.at[t, 0])
 
     @pl.when(pipe < lax.axis_size("pipe") - 1)
     def _():
@@ -325,54 +384,57 @@
 
 def on_device(in_flight, fresh_batch, norm_gain, up_weight, down_weight, expert_ids, route_prob):
     ids = jnp.swapaxes(expert_ids[:, 0], 1, 2)
-    ids = jnp.concatenate([ids, ids], axis=2)
     prob = jnp.swapaxes(route_prob[:, 0], 1, 2)
-    prob = jnp.concatenate([prob, prob], axis=2)
-    vmem = pl.BlockSpec(memory_space=pltpu.VMEM)
     hbm = pl.BlockSpec(memory_space=pl.ANY)
     dma = pltpu.SemaphoreType.DMA
     scratch = [
-        pltpu.VMEM((D, HID), BF16), pltpu.VMEM((HID, D), BF16),
+        pltpu.VMEM((TOK, D), BF16),
+        pltpu.VMEM(fresh_batch.shape, BF16),
+        pltpu.VMEM((1, D), F32),
+        pltpu.VMEM((D, HID), BF16),
+        pltpu.VMEM((HID, D), BF16),
+        pltpu.VMEM((TICKS, TOPK, TOK), jnp.int32),
+        pltpu.VMEM((TICKS, TOPK, TOK), F32),
         pltpu.VMEM((TICKS, NC, 512, C), BF16),
         pltpu.VMEM((TICKS, NC, 4, SIDE, 16, C), BF16),
         pltpu.VMEM((TICKS, NC, SIDE, 16, C2), BF16),
-        pltpu.VMEM((TICKS, NC, SIDE, 4, 16, C), BF16),
+        pltpu.VMEM((TICKS, NC, 4, SIDE, 16, C), BF16),
         pltpu.VMEM((TICKS, NC, SIDE, 16, C2), BF16),
-        pltpu.VMEM((576, HID), F32),
-        pltpu.VMEM((TICKS, HC, 576, HW), BF16),
-        pltpu.VMEM((TICKS, HC, 576, HW), BF16),
-        pltpu.VMEM((576, HID), BF16),
-        pltpu.VMEM((TICKS, NC, SIDE, 4, 16, C), BF16),
+        pltpu.VMEM((TICKS, 4, 128, HID), BF16),
+        pltpu.VMEM((TICKS, 4, 128, HID), BF16),
+        pltpu.VMEM((TICKS, 64, HID), BF16),
+        pltpu.VMEM((TICKS, 64, HID), BF16),
+        pltpu.VMEM((TICKS, NC, 4, SIDE, 16, C), BF16),
         pltpu.VMEM((TICKS, NC, SIDE, 16, C2), BF16),
         pltpu.VMEM((TICKS, NC, 4, SIDE, 16, C), BF16),
         pltpu.VMEM((TICKS, NC, SIDE, 16, C2), BF16),
+        pltpu.VMEM((NC, 64, C), BF16),
         pltpu.VMEM((TICKS, NC, SIDE, TOK, C), BF16),
         pltpu.VMEM((TICKS, NC, SIDE, TOK, C), BF16),
         pltpu.VMEM((TICKS, TOK, 128), F32),
         pltpu.VMEM((TICKS, TOK, 128), F32),
         pltpu.VMEM((TICKS, NC, TOK, C), BF16),
         pltpu.VMEM((TICKS, NC, TOK, C), BF16),
-        pltpu.VMEM((TOK, D), BF16),
         pltpu.VMEM((SIDE, 32, 128), F32),
         pltpu.VMEM((SIDE, 32, 128), F32),
         pltpu.VMEM((TICKS, 4, 128, 128), BF16),
         pltpu.VMEM((TICKS, 64, 512), BF16),
         pltpu.VMEM((TICKS, 4, 128, 128), BF16),
         pltpu.VMEM((TICKS, 4, 128, 128), BF16),
-        dma((2,)), dma((2,)), dma((TICKS, 2)), dma((TICKS, NC)), dma((TICKS, NC)),
-        dma((TICKS, NC)), dma((TICKS, NC, SIDE)), dma((TICKS, NC, 2)), dma((TICKS, NC, 2)),
-        dma((TICKS, HC, 2)), dma((TICKS, NC, 2)), dma((TICKS, NC, 2)),
+        dma((7,)), dma((2,)), dma((TICKS, 2)), dma((TICKS, NC)), dma((TICKS, NC)),
+        dma((TICKS, NC)), dma((TICKS, NC, SIDE)), dma((TICKS, NC)), dma((TICKS, NC, 4)), dma((TICKS, NC, 2)),
+        dma((TICKS, 4, 2)), dma((TICKS, 2)), dma((TICKS, NC)), dma((TICKS, NC, 4)), dma((TICKS, NC, 2)),
         dma((TICKS, NC)), dma((TICKS, NC, SIDE)),
     ]
     y = pl.pallas_call(
         kernel,
         name="window",
         out_shape=jax.ShapeDtypeStruct((TOK, D), BF16),
-        in_specs=[vmem, vmem, vmem, hbm, hbm, vmem, vmem],
-        out_specs=vmem,
+        in_specs=[hbm] * 7,
+        out_specs=pl.BlockSpec(memory_space=pltpu.VMEM),
         scratch_shapes=scratch,
         compiler_params=pltpu.CompilerParams(
-            collective_id=0, has_side_effects=True, vmem_limit_bytes=48 * 2**20
+            collective_id=0, has_side_effects=True, vmem_limit_bytes=62 * 2**20
         ),
     )(in_flight[0], fresh_batch, norm_gain, up_weight[0, 0], down_weight[0, 0], ids, prob)
     return y[None]

time: 164 us -> 146 us (0.89)
  Pallas kernels: 156 us -> 144 us
  local copies, waits for them, and re-layouts: 5.97 us -> 1.57 us
  other arithmetic: 1.69 us -> 0 us
    pallas_call x1, Pallas kernels: 156 us -> 144 us  [on_device(): pl.pallas_call(kernel, name='window', out_shape=jax.ShapeDtypeStruct((TOK...]
    unnamed x11 -> x1, local copies, waits for them, and re-layouts: 5.97 us -> 1.57 us
    concatenate x2 -> x0, other arithmetic: 1.69 us -> none  [the longest x1 0.85 us: on_device(): prob = jnp.concatenate([prob, prob], axis=2)]
where the time goes in v2:
time: 146 us
  Pallas kernels  144 us (99%)
  local copies, waits for them, and re-layouts  1.57 us (1%)
    pallas_call x1, Pallas kernels, on_device(): pl.pallas_call(kernel, name='window', out_shape=jax.ShapeDtypeStruct((TOK...  144 us

profile of v2, /device:TPU:14, one launch (start us, length us, event | category | flops | bytes accessed | tf_op | source)
XLA Modules:
  0.0 146.0 jit_solution(7925420663669184952)
XLA Ops:
  0.0 144.4 %window.1 = bf16[64,1024]{1,0:T(8,128)(2,1)} custom-call(bf16[64,1024]{1,0:T(8,128)(2,1)} %bitcast.13, bf16[1,64,1024]{2,1,0:T(8,128)(2,1)} %fresh_hbm.1, f32[1,1024]{1,0:T(1,128)} %gain_hbm.1, bf16[1024,768]{1,0:T(8,128)(2,1)} %bitcast.10, bf16[768,1024]{1,0:T(8,128)(2,1)} %bitcast.11, s32[2,8,64]{2,1,0:T(8,128)} %bitcast.14, f32[2,8,64]{2,1,0:T(8,128)} %bitcast.15), custom_call_target="tpu_custom_call" | custom-call | tf_op jit(solution)/shard_map/window/pallas_call | solution.py:429
  144.4 1.6 %copy.9 = bf16[1,64,1024]{2,1,0:T(8,128)(2,1)} copy(bf16[1,64,1024]{2,1,0:T(8,128)(2,1)} %bitcast.12) | data formatting | bytes 262144

commit v3 on v2

--- a/solution.py
+++ b/solution.py
@@ -23,7 +23,7 @@
 
 OFFSETS = (0, 1, 7, 2, 6, 3, 5, 4)
 POS = {j: p for p, j in enumerate(OFFSETS)}
-PARENT = {1: 0, 2: 1, 3: 2, 4: 3, 7: 0, 6: 7, 5: 6}
+PARENT = {1: 0, 7: 0, 2: 0, 6: 0, 3: 2, 5: 6, 4: 3}
 CHILDREN = {j: tuple(c for c in PARENT if PARENT[c] == j) for j in range(SIDE)}
 ARRIVALS = ((1, 7), (2, 6), (3, 5), (4,))
 FAR_FIRST = (4, 3, 5, 2, 6, 1, 7)
@@ -42,8 +42,8 @@
     x_hbm, fresh_hbm, gain_hbm, up_hbm, down_hbm, ids_hbm, prob_hbm, out_ref,
     xn, fresh_ref, gain_ref, wup, wdn, ids_ref, prob_ref,
     gb, mb, xb, rb, rxb, ps, pr, pse, pre, ob, oxb, tb, txb, te, sb, rr,
-    sqs, sqr, shs, shr, ms, mr, omat, o8, got, g8t,
-    load_sem, meta_sem, sq_sem, sh_send, sh_recv, ring_send, ring_recv, main_send, main_recv, ext_sem,
+    sqs, sqr, sqy, shs, shr, ms, mr, omat, o8, got, g8t,
+    load_sem, meta_sem, sq_sem, sqy_send, sqy_recv, sh_send, sh_recv, ring_send, ring_recv, main_send, main_recv, ext_sem,
     p_sem, pe_sem, rmain_send, rmain_recv, rext_sem, back_send, back_recv,
 ):
     core = lax.axis_index("tensor")
@@ -94,10 +94,12 @@
     @pl.when(pipe > 0)
     def _():
         greet({"pipe": pipe - 1})
+        greet({"pipe": pipe - 1, "tensor": 1 - core})
 
     @pl.when(pipe < lax.axis_size("pipe") - 1)
     def _():
         greet({"pipe": pipe + 1})
+        greet({"pipe": pipe + 1, "tensor": 1 - core})
 
     def put_squares(t, x):
         sums = jnp.sum(x * x, axis=1, keepdims=True)
@@ -105,6 +107,12 @@
 
     def squares_copy(t):
         return remote(sqs.at[t], sqr.at[t], sq_sem.at[t, 0], sq_sem.at[t, 1], other_core)
+
+    def passed_squares(t, by):
+        return (
+            remote(sqy.at[t], sqs.at[t], sqy_send.at[t, 0], sqy_recv.at[t, 0], {"pipe": pipe + by}),
+            remote(sqy.at[t], sqr.at[t], sqy_send.at[t, 1], sqy_recv.at[t, 1], {"pipe": pipe + by, "tensor": 1 - core}),
+        )
 
     def make_meta():
         row = lax.broadcasted_iota(jnp.int32, (SIDE * SIDE, 128), 0)
@@ -129,7 +137,7 @@
             ms[:, 16 * t + 8 : 16 * t + 16, :] = gates.reshape(SIDE, SIDE, 128)
         mr[0] = ms[0]
 
-    def build_maps(t):
+    def build_maps(t, back):
         row = lax.broadcasted_iota(jnp.int32, (128, 128), 0)
         lane = lax.broadcasted_iota(jnp.int32, (128, 128), 1)
         same = (lax.rem(row, 16) // 8) == (lane // TOK)
@@ -137,20 +145,22 @@
         xrow = lax.broadcasted_iota(jnp.int32, (64, 128), 0)
         xlane = lax.broadcasted_iota(jnp.int32, (64, 128), 1)
         low = lax.broadcasted_iota(jnp.int32, (8, 128), 1) < TOK
+
+        def widen(rows, times):
+            return jnp.concatenate([jnp.broadcast_to(rows[i : i + 1], (times, 128)) for i in range(8)], axis=0)
+
         for q in range(4):
             slots = jnp.where(low, mr[2 * q, 16 * t : 16 * t + 8, :], mr[2 * q + 1, 16 * t : 16 * t + 8, :])
-            gates = jnp.where(low, mr[2 * q, 16 * t + 8 : 16 * t + 16, :], mr[2 * q + 1, 16 * t + 8 : 16 * t + 16, :])
-            wide = jnp.concatenate([jnp.broadcast_to(slots[i : i + 1], (16, 128)) for i in range(8)], axis=0)
-            wide_gate = jnp.concatenate([jnp.broadcast_to(gates[i : i + 1], (16, 128)) for i in range(8)], axis=0)
-            hit = same & (wide == slot)
-            omat[t, q] = jnp.where(hit, 1.0, 0.0).astype(BF16)
-            got[t, q] = jnp.where(hit, wide_gate, 0.0).T.astype(BF16)
-            wide = jnp.concatenate([jnp.broadcast_to(slots[i : i + 1], (8, 128)) for i in range(8)], axis=0)
-            wide_gate = jnp.concatenate([jnp.broadcast_to(gates[i : i + 1], (8, 128)) for i in range(8)], axis=0)
-            hit = (lax.rem(xrow, 8) == 2 * q + xlane // TOK) & (wide == 8.0)
-            o8[t, :, 128 * q : 128 * q + 128] = jnp.where(hit, 1.0, 0.0).astype(BF16)
-            spread_gate = jnp.concatenate([jnp.where(hit, wide_gate, 0.0), jnp.zeros((64, 128), F32)], axis=0)
-            g8t[t, q] = spread_gate.T.astype(BF16)
+            hit = same & (widen(slots, 16) == slot)
+            extra_hit = (lax.rem(xrow, 8) == 2 * q + xlane // TOK) & (widen(slots, 8) == 8.0)
+            if back:
+                gates = jnp.where(low, mr[2 * q, 16 * t + 8 : 16 * t + 16, :], mr[2 * q + 1, 16 * t + 8 : 16 * t + 16, :])
+                got[t, q] = jnp.where(hit, widen(gates, 16), 0.0).T.astype(BF16)
+                spread_gate = jnp.concatenate([jnp.where(extra_hit, widen(gates, 8), 0.0), jnp.zeros((64, 128), F32)], axis=0)
+                g8t[t, q] = spread_gate.T.astype(BF16)
+            else:
+                omat[t, q] = jnp.where(hit, 1.0, 0.0).astype(BF16)
+                o8[t, :, 128 * q : 128 * q + 128] = jnp.where(extra_hit, 1.0, 0.0).astype(BF16)
 
     def pack_extra(rows, ref):
         for p in range(SIDE):
@@ -169,7 +179,7 @@
     ids_load.wait()
     prob_load.wait()
     make_meta()
-    greeted = 2 * (SIDE - 1) + 1 + jnp.where(pipe > 0, 1, 0) + jnp.where(pipe < lax.axis_size("pipe") - 1, 1, 0)
+    greeted = 2 * (SIDE - 1) + 1 + jnp.where(pipe > 0, 2, 0) + jnp.where(pipe < lax.axis_size("pipe") - 1, 2, 0)
     pl.semaphore_wait(barrier, greeted)
     squares_copy(0).start()
     for j in range(1, SIDE):
@@ -177,10 +187,14 @@
     gain_load.wait()
 
     for t in range(TICKS):
-        if t > 0:
-            put_squares(t, xn[...].astype(F32))
-            squares_copy(t).start()
-        squares_copy(t).wait()
+        if t == 0:
+            squares_copy(t).wait()
+        else:
+            @pl.when(pipe > 0)
+            def _():
+                for copy in passed_squares(t, -1):
+                    copy.wait_recv()
+
         scale = lax.rsqrt((sqs[t] + sqr[t]) / (2.0 * D) + EPS)[:, :1]
 
         def ring_copy(k, j):
@@ -197,7 +211,7 @@
                 ring_copy(k, j).start()
         if t == 0:
             remote(mr.at[pl.ds(1, 7)], mr.at[pl.ds(1, 7)], meta_sem.at[0], meta_sem.at[1], first(1)).wait_recv()
-            build_maps(t)
+            build_maps(0, False)
 
         def main_copy(k, q, i):
             p = POS[i]
@@ -253,8 +267,10 @@
             if step >= 2:
                 up_rows(step - 2)
         if t == 0:
+            build_maps(0, True)
             for later in range(1, TICKS):
-                build_maps(later)
+                build_maps(later, False)
+                build_maps(later, True)
         up_rows(2)
         up_rows(3)
         up_extra()
@@ -300,6 +316,7 @@
             )
 
         def sum_pair(q):
+            squares = jnp.zeros((TOK, 1), F32)
             for k in range(NC):
                 if q == 3:
                     seven = txb.at[t, k, pl.ds(1, 7)]
@@ -330,6 +347,15 @@
                             def _():
                                 remote(shs.at[t, k], shr.at[t, k], sh_send.at[t, k], sh_recv.at[t, k], {"pipe": pipe + 1}).start()
 
+                            squares = squares + jnp.sum(y.astype(F32) * y.astype(F32), axis=1, keepdims=True)
+                            if k == NC - 1:
+                                sqy[t + 1] = jnp.broadcast_to(squares, (TOK, 128))
+
+                                @pl.when(pipe < lax.axis_size("pipe") - 1)
+                                def _():
+                                    for copy in passed_squares(t + 1, 1):
+                                        copy.start()
+
         down_extra()
         down_rows(3)
         down_rows(2)
@@ -353,6 +379,9 @@
             @pl.when(pipe == 0)
             def _():
                 xn[...] = fresh_ref[t]
+                put_squares(t + 1, fresh_ref[t].astype(F32))
+                squares_copy(t + 1).start()
+                squares_copy(t + 1).wait()
 
     seven = pl.ds(1, 7)
 
@@ -378,6 +407,8 @@
     @pl.when(pipe < lax.axis_size("pipe") - 1)
     def _():
         for t in range(TICKS - 1):
+            for copy in passed_squares(t + 1, 1):
+                copy.wait_send()
             for k in range(NC):
                 remote(shs.at[t, k], shr.at[t, k], sh_send.at[t, k], sh_recv.at[t, k], {"pipe": pipe + 1}).wait_send()
 
@@ -413,6 +444,7 @@
         pltpu.VMEM((TICKS, NC, SIDE, TOK, C), BF16),
         pltpu.VMEM((TICKS, TOK, 128), F32),
         pltpu.VMEM((TICKS, TOK, 128), F32),
+        pltpu.VMEM((TICKS, TOK, 128), F32),
         pltpu.VMEM((TICKS, NC, TOK, C), BF16),
         pltpu.VMEM((TICKS, NC, TOK, C), BF16),
         pltpu.VMEM((SIDE, 32, 128), F32),
@@ -421,7 +453,7 @@
         pltpu.VMEM((TICKS, 64, 512), BF16),
         pltpu.VMEM((TICKS, 4, 128, 128), BF16),
         pltpu.VMEM((TICKS, 4, 128, 128), BF16),
-        dma((7,)), dma((2,)), dma((TICKS, 2)), dma((TICKS, NC)), dma((TICKS, NC)),
+        dma((7,)), dma((2,)), dma((TICKS, 2)), dma((TICKS, 2)), dma((TICKS, 2)), dma((TICKS, NC)), dma((TICKS, NC)),
         dma((TICKS, NC)), dma((TICKS, NC, SIDE)), dma((TICKS, NC)), dma((TICKS, NC, 4)), dma((TICKS, NC, 2)),
         dma((TICKS, 4, 2)), dma((TICKS, 2)), dma((TICKS, NC)), dma((TICKS, NC, 4)), dma((TICKS, NC, 2)),
         dma((TICKS, NC)), dma((TICKS, NC, SIDE)),

time: 146 us -> 142 us (0.973)
  Pallas kernels: 144 us -> 139 us
    pallas_call x1, Pallas kernels: 144 us -> 139 us  [on_device(): pl.pallas_call(kernel, name='window', out_shape=jax.ShapeDtypeStruct((TOK...]
where the time goes in v3:
time: 142 us; the launch traced here: 141 us
  Pallas kernels  139 us (98%)
  local copies, waits for them, and re-layouts  1.57 us (1%)
    pallas_call x1, Pallas kernels, on_device(): pl.pallas_call(kernel, name='window', out_shape=jax.ShapeDtypeStruct((TOK...  139 us

profile of v3, /device:TPU:14, one launch (start us, length us, event | category | flops | bytes accessed | tf_op | source)
XLA Modules:
  0.0 140.6 jit_solution(17802128026355981215)
XLA Ops:
  0.0 139.1 %window.1 = bf16[64,1024]{1,0:T(8,128)(2,1)} custom-call(bf16[64,1024]{1,0:T(8,128)(2,1)} %bitcast.13, bf16[1,64,1024]{2,1,0:T(8,128)(2,1)} %fresh_hbm.1, f32[1,1024]{1,0:T(1,128)} %gain_hbm.1, bf16[1024,768]{1,0:T(8,128)(2,1)} %bitcast.10, bf16[768,1024]{1,0:T(8,128)(2,1)} %bitcast.11, s32[2,8,64]{2,1,0:T(8,128)} %bitcast.14, f32[2,8,64]{2,1,0:T(8,128)} %bitcast.15), custom_call_target="tpu_custom_call" | custom-call | tf_op jit(solution)/shard_map/window/pallas_call | solution.py:461
  139.1 1.6 %copy.9 = bf16[1,64,1024]{2,1,0:T(8,128)(2,1)} copy(bf16[1,64,1024]{2,1,0:T(8,128)(2,1)} %bitcast.12) | data formatting | bytes 262144

commit v4 on v3

--- a/solution.py
+++ b/solution.py
@@ -32,6 +32,11 @@
 def offset_of(position):
     odd = lax.rem(position, 2) == 1
     return jnp.where(odd, (position + 1) // 2, lax.rem(SIDE - position // 2, SIDE))
+
+
+def silu(v):
+    half = 0.5 * v
+    return half + half * jnp.tanh(half)
 
 
 def dot(a, b):
@@ -286,7 +291,7 @@
 
         def down_extra():
             total = pse[t].astype(F32) + dot(swap, pre[t])
-            hidden = (total / (1.0 + jnp.exp(-total))).astype(BF16)
+            hidden = silu(total).astype(BF16)
             made = dot(hidden, wdn[...])
             for k in range(NC):
                 pack_extra(made[:, k * C : k * C + C], oxb.at[t, k])
@@ -301,7 +306,7 @@
                 block = pr[t, n, 32 * q : 32 * q + 32].astype(F32)
                 parts += [block[:8], block[16:24], block[8:16], block[24:]]
             total = ps[t, q].astype(F32) + jnp.concatenate(parts, axis=0)
-            hidden = (total / (1.0 + jnp.exp(-total))).astype(BF16)
+            hidden = silu(total).astype(BF16)
             for k in range(NC):
                 made = dot(hidden, wdn[:, k * C : k * C + C]).astype(BF16).reshape(SIDE, 16, C)
                 ob[t, k, q] = made
@@ -359,10 +364,10 @@
         down_extra()
         down_rows(3)
         down_rows(2)
+        down_rows(1)
         sum_pair(3)
-        down_rows(1)
+        down_rows(0)
         sum_pair(2)
-        down_rows(0)
         sum_pair(1)
         sum_pair(0)
 

time: 142 us -> 142 us (level)
  no operation moved by 1% of the time
where the time goes in v4:
time: 142 us
  Pallas kernels  140 us (99%)
  local copies, waits for them, and re-layouts  1.57 us (1%)
    pallas_call x1, Pallas kernels, on_device(): pl.pallas_call(kernel, name='window', out_shape=jax.ShapeDtypeStruct((TOK...  140 us

profile of v4, /device:TPU:14, one launch (start us, length us, event | category | flops | bytes accessed | tf_op | source)
XLA Modules:
  0.0 141.7 jit_solution(2882152937014812846)
XLA Ops:
  0.0 140.1 %window.1 = bf16[64,1024]{1,0:T(8,128)(2,1)} custom-call(bf16[64,1024]{1,0:T(8,128)(2,1)} %bitcast.13, bf16[1,64,1024]{2,1,0:T(8,128)(2,1)} %fresh_hbm.1, f32[1,1024]{1,0:T(1,128)} %gain_hbm.1, bf16[1024,768]{1,0:T(8,128)(2,1)} %bitcast.10, bf16[768,1024]{1,0:T(8,128)(2,1)} %bitcast.11, s32[2,8,64]{2,1,0:T(8,128)} %bitcast.14, f32[2,8,64]{2,1,0:T(8,128)} %bitcast.15), custom_call_target="tpu_custom_call" | custom-call | tf_op jit(solution)/shard_map/window/pallas_call | solution.py:466
  140.1 1.6 %copy.9 = bf16[1,64,1024]{2,1,0:T(8,128)(2,1)} copy(bf16[1,64,1024]{2,1,0:T(8,128)(2,1)} %bitcast.12) | data formatting | bytes 262144
